TPU v7x, 32 devices: a whole 2x2x4 slice. The times are simulated.
32 devices in a mesh: groups: 2 (over x), row: 16 (over z, y, core).
Axes of the slice: x: 2, y: 2, z: 4, core: 2. Of those that a mesh axis runs over, the one named last changes fastest.
Arguments:
- design_rows: float32 [512, 8192], P(('groups', 'row')), parts along dimension 0, may hold values from -1.5 to 1.5
- arc_ids: int32 [512], P(('groups', 'row')), parts along dimension 0, may hold values from 0 to 3, never falling along the last dimension, each value on 1 to 128 neighbouring positions
- tile_order: int32 [64], replicated, may hold values from 0 to 63, each once
Outputs:
- normal_slab: float32 [5888, 8192], P('groups', 'row'), parts along dimension 0
There are 2 independent parts, one for each index of `groups`. A program takes and returns all parts, laid end to end along the dimension named above; an argument that names none is the same for every part. Nothing has to cross between parts.
Inputs may be any that keep to these rules, and one draw needn't show every extreme that they name: `arc_ids`: arc ids never fall along the observations; each arc holds 1 to 128 consecutive observations, and some arc exactly 128. `tile_order`: each column tile appears once.
All inputs are finite; a program needn't handle non-finite values.
Results may differ from a plain program's by a relative error of at most 0.000086.
Values sent between devices are 32-bit elements; how exact they have to be, the bound alone decides.
A program may use at most 128 MiB of HBM per device.

v0:
```python
import jax
import jax.numpy as jnp
from jax import lax
from jax.sharding import PartitionSpec as P

SLAB = 2944
TILE = 128


def entering(value, axis, join, neutral, backward):
    count, mine = (lax.axis_size(axis), lax.axis_index(axis))
    pieces = jax.tree.map(lambda part: lax.all_gather(part, axis), value)
    if backward:
        pieces = jax.tree.map(lambda part: part[::-1], pieces)
        mine = count - 1 - mine
    subtotal = jax.tree.map(
        lambda part, zero: jnp.full_like(part, 0) + jnp.asarray(zero, part.dtype), value, neutral
    )

    def lap(position, subtotal):
        longer = join(subtotal, jax.tree.map(lambda part: part[position], pieces))
        return jax.tree.map(lambda new, old: jnp.where(position < mine, new, old), longer, subtotal)

    return lax.fori_loop(0, count - 1, lap, subtotal)


def product(left_block, right_block):
    return lax.dot_general(
        left_block,
        right_block,
        (((0,), (0,)), ((), ())),
        precision=lax.Precision.HIGHEST,
        preferred_element_type=jnp.float32,
    )


def join_arcs(earlier, later):
    e_id, e_sum, e_count, e_whole = earlier
    l_id, l_sum, l_count, l_whole = later
    joined = jnp.logical_and(l_whole > 0.5, l_id == e_id)
    out_sum = jnp.where(joined, e_sum + l_sum, l_sum)
    out_count = jnp.where(joined, e_count + l_count, l_count)
    out_whole = jnp.where(joined, e_whole, jnp.where(e_count > 0.5, 0.0, l_whole))
    later_empty = l_count < 0.5
    return (
        jnp.where(later_empty, e_id, l_id),
        jnp.where(later_empty, e_sum, out_sum),
        jnp.where(later_empty, e_count, out_count),
        jnp.where(later_empty, e_whole, out_whole),
    )


def shards(design_rows, arc_ids, tile_order):
    obs_local, total_cols = design_rows.shape
    peers = lax.axis_size("row")
    first_id = arc_ids[0]
    last_id = arc_ids[obs_local - 1]
    relative = arc_ids - first_id
    labels = jnp.arange(obs_local, dtype=jnp.int32)
    onehot = (relative[:, None] == labels[None, :]).astype(jnp.float32)
    local_counts = jnp.sum(onehot, axis=0)
    local_sums = product(onehot, design_rows)
    tail_slot = last_id - first_id
    tail_pick = (labels == tail_slot).astype(jnp.float32)
    head_pick = (labels == 0).astype(jnp.float32)
    tail_sum = jnp.dot(tail_pick, local_sums, precision=lax.Precision.HIGHEST)
    tail_count = jnp.sum(tail_pick * local_counts)
    head_sum = local_sums[0]
    head_count = local_counts[0]
    whole_one = jnp.where(first_id == last_id, 1.0, 0.0).astype(jnp.float32)
    first_f = first_id.astype(jnp.float32)
    last_f = last_id.astype(jnp.float32)
    identity = (
        jnp.float32(-1.0),
        jnp.zeros((total_cols,), jnp.float32),
        jnp.float32(0.0),
        jnp.float32(1.0),
    )
    from_left = entering(
        (last_f, tail_sum, tail_count, whole_one), "row", join_arcs, identity, False
    )
    from_right = entering(
        (first_f, head_sum, head_count, whole_one), "row", join_arcs, identity, True
    )
    left_match = jnp.where(from_left[0] == first_f, 1.0, 0.0) * head_pick
    right_match = jnp.where(from_right[0] == last_f, 1.0, 0.0) * tail_pick
    arc_sums = (
        local_sums
        + left_match[:, None] * from_left[1][None, :]
        + right_match[:, None] * from_right[1][None, :]
    )
    arc_counts = local_counts + left_match * from_left[2] + right_match * from_right[2]
    arc_means = arc_sums / jnp.maximum(arc_counts, 1.0)[:, None]
    centered = design_rows - jnp.dot(
        onehot, arc_means, precision=lax.Precision.HIGHEST, preferred_element_type=jnp.float32
    )
    owned_local = centered.reshape(obs_local, total_cols // TILE, TILE)[:, tile_order, :]
    owned_local = owned_local.reshape(obs_local, peers, total_cols // peers)
    slab_local = centered[:, :SLAB]
    mine = lax.all_to_all(owned_local, "row", split_axis=1, concat_axis=0, tiled=True)[:, 0, :]
    slab_all = lax.all_gather(slab_local, "row", axis=0, tiled=True)
    normal_slab = product(slab_all, mine)
    return normal_slab


def solution(mesh):
    return jax.shard_map(
        shards,
        mesh=mesh,
        in_specs=(P(("groups", "row"), None), P(("groups", "row")), P()),
        out_specs=P("groups", "row"),
        check_vma=False,
    )
```

profile of v0, /device:TPU:0, one launch (start us, length us, event | category | flops | bytes accessed | tf_op | source)
XLA Modules:
  0.0 344.1 jit_solution(16535701577360113606)
XLA Ops:
  6.5 1.3 fusion.18
  11.7 1.3 broadcast_subtract_fusion
  13.1 1.5 fusion.10
  15.6 1.2 dynamic-slice
  16.8 0.7 slice_dynamic-update-slice_fusion
  17.6 0.8 dynamic-update-slice.2
  18.3 0.8 dynamic-update-slice.1
  19.1 0.8 dynamic-update-slice.4
  19.8 1.4 dynamic-update-slice
  21.2 35.0 %all-reduce.5 = (f32[16]{0:T(128)S(1)}, f32[16]{0:T(128)S(1)}, f32[16]{0:T(128)S(1)}, f32[16]{0:T(128)S(1)}, f32[16]{0:T(128)S(1)}) all-reduce(f32[16]{0:T(128)S(1)} %slice_dynamic-update-slice_fusion, f32[16]{0:T(128)S(1)} %dynamic-update-slice.4, f32[16]{0:T(128)S(1)} %dynamic-update-slice.2, ...), channel_id=1, replica_groups=mesh['groups'=2,'row'=16] {'row'}, use_global_device_ids=true, to_apply=%add.3 | all-reduce | flops 80 | bytes 640
  56.5 18.7 %all-gather = f32[131072]{0:T(1024)S(1)} all-gather(f32[8192]{0:T(1024)S(1)} %bitcast.60), channel_id=2, replica_groups=mesh['groups'=2,'row'=16] {'row'}, dimensions={0}, use_global_device_ids=true | all-gather | bytes 557056 | tf_op jit(solution)/shard_map/all_gather | solution.py:12
  75.3 87.1 %while.36 = (s32[]{:T(128)}, f32[]{:T(128)}, f32[8192]{0:T(1024)S(1)}, f32[]{:T(128)}, s32[]{:T(128)}, /*index=5*/f32[16]{0:T(128)S(1)}, f32[16]{0:T(128)S(1)}, ...) while((s32[]{:T(128)}, f32[]{:T(128)}, ...), condition=%wide.region_3.4_spmd.clone, body=%wide.region_2.3_spmd.clone.sunk | while | flops 40974 | bytes 164142 | solution.py:24
  162.5 21.0 %all-gather.1 = f32[16,1,8192]{2,1,0:T(1,128)S(1)} all-gather(f32[1,1,8192]{2,1,0:T(1,128)S(1)} %slice_bitcast_fusion), channel_id=1, replica_groups=mesh['groups'=2,'row'=16] {'row'}, dimensions={0}, use_global_device_ids=true | all-gather | bytes 557056 | tf_op jit(solution)/shard_map/all_gather | solution.py:12
  183.8 1.0 rev.15
  184.8 90.9 %while.37 = (s32[]{:T(128)}, f32[]{:T(128)}, f32[8192]{0:T(1024)S(1)}, f32[]{:T(128)}, s32[]{:T(128)}, /*index=5*/f32[16]{0:T(128)S(1)}, f32[16]{0:T(128)S(1)}, ...) while((s32[]{:T(128)}, f32[]{:T(128)}, ...), condition=%wide.region_5.6_spmd.clone, body=%wide.region_4.5_spmd.clone.sunk | while | flops 40974 | bytes 164142 | solution.py:24
  186.7 0.7 dynamic_slice.80
  188.8 0.7 dynamic_slice.81
  192.8 0.7 dynamic_slice.80
  198.8 0.7 dynamic_slice.80
  206.9 0.7 dynamic_slice.81
  213.0 0.7 dynamic_slice.81
  223.1 0.7 dynamic_slice.80
  231.2 0.7 dynamic_slice.81
  237.3 0.7 dynamic_slice.81
  247.3 0.7 dynamic_slice.80
  255.4 0.7 dynamic_slice.81
  265.5 0.7 dynamic_slice.80
  271.6 0.7 dynamic_slice.80
  276.3 0.7 slice.23
  278.3 22.5 %all_to_all.15 = f32[16,16,512]{2,0,1:T(8,128)S(1)} all-to-all(f32[16,16,512]{2,0,1:T(8,128)S(1)} %copy.13), channel_id=1, replica_groups=mesh['groups'=2,'row'=16] {'row'}, dimensions={1} | all-to-all | bytes 1048576 | tf_op jit(solution)/shard_map/all_to_all | solution.py:100
  300.8 23.2 %all-gather.4.cloned.1.call-done = f32[256,2944]{1,0:T(8,128)} async-done(((f32[16,2944]{1,0:T(8,128)}), f32[256,2944]{1,0:T(8,128)}) %all-gather.4.cloned.1.call-update) | async-done | bytes 3014672 | tf_op jit(solution)/shard_map/all_gather | solution.py:101
  324.0 13.2 %fusion.19 = f32[2944,512]{1,0:T(8,128)} fusion(f32[256,2944]{1,0:T(8,128)} %all-gather.4.cloned.1.call-done, f32[256,512]{1,0:T(8,128)S(1)} %bitcast.57), kind=kOutput, calls=%fused_computation.39 | convolution fusion | flops 4630511616 | bytes 9568256 | tf_op jit(solution)/shard_map/dot_general | solution.py:28
  (168 shorter events, 54.0 us)
Async XLA Ops:
  6.5 317.5 %all-gather.4.cloned.1.call-start = ((), (), s32[]{:S(2)}) async-start(), calls=%async_computation.1 | async-start | bytes 3203072 | tf_op jit(solution)/shard_map/all_gather | solution.py:101
  75.2 200.5 %copy-start = (f32[16,8192]{1,0:T(8,128)S(1)}, f32[16,8192]{1,0:T(8,128)}, u32[]{:S(2)}) copy-start(f32[16,8192]{1,0:T(8,128)} %param.7) | copy-start | bytes 1572868
  183.5 93.6 %copy-start.1 = (s32[64]{0:T(128)S(1)}, s32[64]{0:T(128)}, u32[]{:S(2)}) copy-start(s32[64]{0:T(128)} %param.9) | copy-start | bytes 772
Sparse Core Ops, SparseCore 0:
  277.1 46.8 all-gather.3
where the time goes:
time: 346 us; the launch traced here: 344 us
  loops' own time  119 us (34%)
  blocking collectives  97.2 us (28%)
  local copies, waits for them, and re-layouts  69.2 us (20%)
  waiting for transfers between devices  23.2 us (7%)
  between operations  17.4 us (5%)
  matrix products  15.5 us (4%)
    another operation x2, loops' own time, entering(): return lax.fori_loop(0, count - 1, lap, subtotal)  119 us
    dynamic_slice x120, local copies, waits for them, and re-layouts, lap(): longer = join(subtotal, jax.tree.map(lambda part: part[position], pieces))  58.6 us
    all_gather x2, blocking collectives, entering(): pieces = jax.tree.map(lambda part: lax.all_gather(part, axis), value)  39.7 us
    unnamed x1, blocking collectives  35 us
    all_gather x1, waiting for transfers between devices, shards(): slab_all = lax.all_gather(slab_local, 'row', axis=0, tiled=True)  23.2 us
    all_to_all x1, blocking collectives, shards(): lax.all_to_all(owned_local, 'row', split_axis=1, concat_axis=0, tiled=True)  22.5 us
    dot_general x2, matrix products, product(): lax.dot_general(left_block, right_block, (((0,), (0,)), ((), ())), precis...  14.7 us
  transfers between devices with their start and end apart: 1, of which 1 were waited for; matrix products, arithmetic and copies ran while one was open for 0% of the time, Pallas kernels for 0%

commit v1 on v0

v1 whole, which is shorter than its diff:
```python
import functools

import jax
import jax.numpy as jnp
from jax import lax
from jax.experimental import pallas as pl
from jax.experimental.pallas import tpu as pltpu
from jax.sharding import PartitionSpec as P

SLAB = 2944
TILE = 128
WIDE = SLAB + TILE
STEP = 384
CORES = 2
MESH = pl.DeviceIdType.MESH


def exchange(
    depth, order, ids, rows, slab_all, own_all,
    stage, packed, slab_recv, own_recv, slab_send, own_send, local_sem,
):
    me = lax.axis_index("row")
    n = lax.axis_size("row")
    obs = rows.shape[0]
    tiles = packed.shape[2] // TILE
    lane = depth * CORES
    layers = n // lane
    z, inner = me // lane, me % lane
    y, core = inner // CORES, inner % CORES

    barrier = pltpu.get_barrier_semaphore()

    @pl.loop(1, n)
    def _(hop):
        pl.semaphore_signal(
            barrier, inc=1, device_id={"row": lax.rem(me + hop, n)}, device_id_type=MESH
        )

    stage[:, :SLAB] = rows[:, :SLAB]
    for obs_at in range(obs):
        value = ids[obs_at].astype(jnp.float32)
        stage[obs_at : obs_at + 1, SLAB:] = jnp.full((1, TILE), value, jnp.float32)

    def at(layer, side, unit):
        return (layer * depth + side) * CORES + unit

    def pass_on(kind, origin, target, own=False):
        return pltpu.make_async_remote_copy(
            src_ref=stage if own else slab_all.at[origin],
            dst_ref=slab_all.at[origin],
            send_sem=slab_send.at[kind, origin],
            recv_sem=slab_recv.at[origin],
            device_id={"row": target},
            device_id_type=MESH,
        )

    up, down = at(z + 1, y, core), at(z - 1, y, core)
    across, twin = at(z, depth - 1 - y, core), at(z, y, CORES - 1 - core)

    def arrived(origin):
        pltpu.make_async_remote_copy(
            src_ref=stage, dst_ref=slab_all.at[origin], send_sem=slab_send.at[0, origin],
            recv_sem=slab_recv.at[origin], device_id={"row": twin}, device_id_type=MESH,
        ).wait_recv()

    pl.semaphore_wait(barrier, n - 1)

    @pl.when(z + 1 < layers)
    def _():
        pass_on(0, me, up, True).start()

    @pl.when(z > 0)
    def _():
        pass_on(1, me, down, True).start()

    if depth > 1:
        pass_on(2, me, across, True).start()
    pass_on(3, me, twin, True).start()
    keep = pltpu.make_async_copy(stage, slab_all.at[me], local_sem.at[0])
    keep.start()

    def pack(peer):
        for k in range(tiles):
            column = order[peer * tiles + k] * TILE
            packed[peer, :, k * TILE : (k + 1) * TILE] = rows[:, pl.ds(column, TILE)]

    def deal(peer):
        return pltpu.make_async_remote_copy(
            src_ref=packed.at[peer],
            dst_ref=own_all.at[me],
            send_sem=own_send.at[peer],
            recv_sem=own_recv.at[me],
            device_id={"row": peer},
            device_id_type=MESH,
        )

    @pl.loop(1, n)
    def _(hop):
        peer = lax.rem(me + hop, n)
        pack(peer)
        deal(peer).start()

    pack(me)
    keep_own = pltpu.make_async_copy(packed.at[me], own_all.at[me], local_sem.at[1])
    keep_own.start()

    @pl.loop(1, layers + 1)
    def _(s):
        @pl.when(z - s >= 0)
        def _():
            origin = at(z - s, y, core)
            arrived(origin)

            @pl.when(z + 1 < layers)
            def _():
                pass_on(0, origin, up).start()

            if depth > 1:
                pass_on(2, origin, across).start()
            pass_on(3, origin, twin).start()

        @pl.when(z + s < layers)
        def _():
            origin = at(z + s, y, core)
            arrived(origin)

            @pl.when(z > 0)
            def _():
                pass_on(1, origin, down).start()

            if depth > 1:
                pass_on(2, origin, across).start()
            pass_on(3, origin, twin).start()

        if depth > 1:
            @pl.when(z - s + 1 >= 0)
            def _():
                origin = at(z - s + 1, depth - 1 - y, core)
                arrived(origin)
                pass_on(3, origin, twin).start()

            @pl.when(jnp.logical_and(s > 1, z + s - 1 < layers))
            def _():
                origin = at(z + s - 1, depth - 1 - y, core)
                arrived(origin)
                pass_on(3, origin, twin).start()

    @pl.loop(0, layers)
    def _(layer):
        for side in range(depth):
            arrived(at(layer, side, CORES - 1 - core))

    @pl.loop(1, n)
    def _(hop):
        peer = lax.rem(me + hop, n)
        pltpu.make_async_remote_copy(
            src_ref=packed.at[peer], dst_ref=own_all.at[peer], send_sem=own_send.at[peer],
            recv_sem=own_recv.at[peer], device_id={"row": peer}, device_id_type=MESH,
        ).wait()

    keep.wait()
    keep_own.wait()

    @pl.loop(0, layers)
    def _(layer):
        origin = at(layer, y, core)

        @pl.when(jnp.logical_and(layer <= z, z + 1 < layers))
        def _():
            pass_on(0, origin, up).wait_send()

        @pl.when(jnp.logical_and(layer >= z, z > 0))
        def _():
            pass_on(1, origin, down).wait_send()

        if depth > 1:
            pass_on(2, origin, across).wait_send()
        for side in range(depth):
            pass_on(3, at(layer, side, core), twin).wait_send()


def two(value):
    high = value.astype(jnp.bfloat16)
    return high, (value - high.astype(jnp.float32)).astype(jnp.bfloat16)


def dot(left, right, over=1):
    return lax.dot_general(
        left, right, (((over,), (0,)), ((), ())), preferred_element_type=jnp.float32
    )


def normal(id_ref, own_ref, slab_ref, out_ref, same, counts, own_high, own_low):
    @pl.when(pl.program_id(0) == 0)
    def _():
        arcs = id_ref[...]
        across = jnp.transpose(arcs)[0:1, :]
        alike = (arcs[:, 0:1] == across).astype(jnp.float32)
        same[...] = alike.astype(jnp.bfloat16)
        counts[...] = jnp.broadcast_to(jnp.sum(alike, axis=1, keepdims=True), counts.shape)
        own = own_ref[...]
        high, rest = two(own)
        middle, low = two(own - high.astype(jnp.float32))
        mask = same[...]
        sums = dot(mask, low) + dot(mask, middle) + dot(mask, high)
        centered = own - sums / counts[:, 0:1]
        own_high[...], own_low[...] = two(centered)

    slab = slab_ref[...]
    shift = dot(same[...], slab.astype(jnp.bfloat16)) / counts[:, 0:1]
    high, low = two(jnp.transpose(slab - shift))
    out_ref[...] = dot(low, own_high[...]) + dot(high, own_low[...]) + dot(high, own_high[...])


def shards(depth, design_rows, arc_ids, tile_order):
    obs, columns = design_rows.shape
    n = lax.axis_size("row")
    mine = columns // n
    total = n * obs
    slab_all, own_all = pl.pallas_call(
        functools.partial(exchange, depth),
        out_shape=(
            jax.ShapeDtypeStruct((n, obs, WIDE), jnp.float32),
            jax.ShapeDtypeStruct((n, obs, mine), jnp.float32),
        ),
        in_specs=[
            pl.BlockSpec(memory_space=pltpu.SMEM),
            pl.BlockSpec(memory_space=pltpu.SMEM),
            pl.BlockSpec(memory_space=pltpu.VMEM),
        ],
        out_specs=(pl.BlockSpec(memory_space=pl.ANY), pl.BlockSpec(memory_space=pl.ANY)),
        scratch_shapes=[
            pltpu.VMEM((obs, WIDE), jnp.float32),
            pltpu.VMEM((n, obs, mine), jnp.float32),
            pltpu.SemaphoreType.DMA((n,)),
            pltpu.SemaphoreType.DMA((n,)),
            pltpu.SemaphoreType.DMA((4, n)),
            pltpu.SemaphoreType.DMA((n,)),
            pltpu.SemaphoreType.DMA((2,)),
        ],
        compiler_params=pltpu.CompilerParams(
            collective_id=0, has_side_effects=True, vmem_limit_bytes=16 << 20
        ),
        name="exchange",
    )(tile_order, arc_ids, design_rows)
    slab_all = slab_all.reshape(total, WIDE)
    own_all = own_all.reshape(total, mine)
    return pl.pallas_call(
        normal,
        grid=(pl.cdiv(SLAB, STEP),),
        out_shape=jax.ShapeDtypeStruct((SLAB, mine), jnp.float32),
        in_specs=[
            pl.BlockSpec((total, TILE), lambda i: (0, SLAB // TILE)),
            pl.BlockSpec((total, mine), lambda i: (0, 0)),
            pl.BlockSpec((total, STEP), lambda i: (0, i)),
        ],
        out_specs=pl.BlockSpec((STEP, mine), lambda i: (i, 0)),
        scratch_shapes=[
            pltpu.VMEM((total, total), jnp.bfloat16),
            pltpu.VMEM((total, TILE), jnp.float32),
            pltpu.VMEM((total, mine), jnp.bfloat16),
            pltpu.VMEM((total, mine), jnp.bfloat16),
        ],
        compiler_params=pltpu.CompilerParams(vmem_limit_bytes=40 << 20),
        name="normal",
    )(slab_all, own_all, slab_all)


def solution(mesh):
    depth = 4 // mesh.shape["groups"]
    return jax.shard_map(
        functools.partial(shards, depth),
        mesh=mesh,
        in_specs=(P(("groups", "row"), None), P(("groups", "row")), P()),
        out_specs=P("groups", "row"),
        check_vma=False,
    )
```

time: 346 us -> 50.6 us (0.15)
  loops' own time: 119 us -> 0 us
  blocking collectives: 97.2 us -> 0 us
  local copies, waits for them, and re-layouts: 69.2 us -> 2.35 us
  Pallas kernels: 0 us -> 47.9 us
  waiting for transfers between devices: 23.2 us -> 0 us
  between operations: 17.4 us -> 0.01 us
  matrix products: 15.5 us -> 0 us
    another operation x2 -> x0, loops' own time: 119 us -> none  [entering(): return lax.fori_loop(0, count - 1, lap, subtotal)]
    dynamic_slice x120 -> x0, local copies, waits for them, and re-layouts: 58.6 us -> none  [lap(): longer = join(subtotal, jax.tree.map(lambda part: part[position], pieces))]
    pallas_call x0 -> x2, Pallas kernels: none -> 47.9 us  [the longest x1 40.1 us: shards(): pl.pallas_call(functools.partial(exchange, depth), out_shape=(jax.ShapeDt...]
    all_gather x2 -> x0, blocking collectives: 39.7 us -> none  [entering(): pieces = jax.tree.map(lambda part: lax.all_gather(part, axis), value)]
    unnamed x1 -> x0, blocking collectives: 35 us -> none
    all_gather x1 -> x0, waiting for transfers between devices: 23.2 us -> none  [shards(): slab_all = lax.all_gather(slab_local, 'row', axis=0, tiled=True)]
    all_to_all x1 -> x0, blocking collectives: 22.5 us -> none  [shards(): lax.all_to_all(owned_local, 'row', split_axis=1, concat_axis=0, tiled=True)]
    dot_general x4 -> x0, matrix products: 15.5 us -> none  [the longest x2 14.7 us: product(): lax.dot_general(left_block, right_block, (((0,), (0,)), ((), ())), precis...]
  transfers between devices with their start and end apart: 1 -> 0, of which waited for: 1 -> 0; matrix products, arithmetic and copies ran while one was open for 0% -> 0% of each run, Pallas kernels for 0% -> 0%
where the time goes in v1:
time: 50.6 us; the launch traced here: 50.2 us
  Pallas kernels  47.9 us (95%)
  local copies, waits for them, and re-layouts  2.35 us (5%)
    pallas_call x1, Pallas kernels, shards(): pl.pallas_call(functools.partial(exchange, depth), out_shape=(jax.ShapeDt...  40.1 us
    pallas_call x1, Pallas kernels, shards(): pl.pallas_call(normal, grid=(pl.cdiv(SLAB, STEP),), out_shape=jax.ShapeDt...  7.8 us
    unnamed x6, local copies, waits for them, and re-layouts  2.35 us

profile of v1, /device:TPU:0, one launch (start us, length us, event | category | flops | bytes accessed | tf_op | source)
XLA Modules:
  0.0 50.2 jit_solution(8464371128467176401)
XLA Ops:
  0.0 0.0 copy-start
  0.0 1.0 %copy-done = f32[16,8192]{1,0:T(8,128)S(1)} copy-done((f32[16,8192]{1,0:T(8,128)S(1)}, f32[16,8192]{1,0:T(8,128)}, u32[]{:S(2)}) %copy-start) | copy-done | bytes 524312
  1.0 0.0 copy-start.1
  1.0 0.7 %copy-done.1 = s32[64]{0:T(128)S(1)} copy-done((s32[64]{0:T(128)S(1)}, s32[64]{0:T(128)}, u32[]{:S(2)}) %copy-start.1) | copy-done | bytes 280
  1.7 0.0 copy-start.2
  1.7 0.7 %copy-done.2 = s32[16]{0:T(128)S(1)} copy-done((s32[16]{0:T(128)S(1)}, s32[16]{0:T(128)}, u32[]{:S(2)}) %copy-start.2) | copy-done | bytes 88
  2.4 40.1 %exchange.1 = (f32[16,16,3072]{2,1,0:T(8,128)S(1)}, f32[16,16,512]{2,1,0:T(8,128)S(1)}) custom-call(s32[64]{0:T(128)S(1)} %copy-done.1, s32[16]{0:T(128)S(1)} %copy-done.2, f32[16,8192]{1,0:T(8,128)S(1)} %copy-done), custom_call_target="tpu_custom_call" | custom-call | tf_op jit(solution)/shard_map/exchange/pallas_call | solution.py:220
  42.4 7.8 %normal.1 = f32[2944,512]{1,0:T(8,128)} custom-call(f32[256,3072]{1,0:T(8,128)S(1)} %bitcast.2, f32[256,512]{1,0:T(8,128)S(1)} %bitcast.4, f32[256,3072]{1,0:T(8,128)S(1)} %bitcast.3), custom_call_target="tpu_custom_call" | custom-call | tf_op jit(solution)/shard_map/normal/pallas_call | solution.py:248
Async XLA Ops:
  0.0 1.0 %copy-start = (f32[16,8192]{1,0:T(8,128)S(1)}, f32[16,8192]{1,0:T(8,128)}, u32[]{:S(2)}) copy-start(f32[16,8192]{1,0:T(8,128)} %rows.1) | copy-start | bytes 1572868
  1.0 0.7 %copy-start.1 = (s32[64]{0:T(128)S(1)}, s32[64]{0:T(128)}, u32[]{:S(2)}) copy-start(s32[64]{0:T(128)} %order.1) | copy-start | bytes 772
  1.7 0.7 %copy-start.2 = (s32[16]{0:T(128)S(1)}, s32[16]{0:T(128)}, u32[]{:S(2)}) copy-start(s32[16]{0:T(128)} %ids.1) | copy-start | bytes 196

commit v2 on v1

v2 whole, which is shorter than its diff:
```python
import functools

import jax
import jax.numpy as jnp
from jax import lax
from jax.experimental import pallas as pl
from jax.experimental.pallas import tpu as pltpu
from jax.sharding import PartitionSpec as P

SLAB = 2944
TILE = 128
WIDE = SLAB + TILE
STEP = 768
PARTS = 2
DEALS = 2
CORES = 2
MESH = pl.DeviceIdType.MESH


def exchange(
    depth, order_in, ids_in, rows_in, slab_all, own_all,
    order, ids, rows, stage, packed, slab_recv, own_recv, slab_send, own_send, load_sem, keep_sem,
    in_below, in_above,
):
    me = lax.axis_index("row")
    n = lax.axis_size("row")
    obs = rows.shape[0]
    tiles = packed.shape[2] // TILE
    lane = depth * CORES
    layers = n // lane
    z, inner = me // lane, me % lane
    y, core = inner // CORES, inner % CORES
    halves, part = obs // 8, WIDE // PARTS
    pieces = halves * PARTS

    loads = [
        pltpu.make_async_copy(rows_in, rows, load_sem.at[0]),
        pltpu.make_async_copy(ids_in, ids, load_sem.at[1]),
        pltpu.make_async_copy(order_in, order, load_sem.at[2]),
    ]
    for load in loads:
        load.start()

    def at(layer, side, unit):
        return (layer * depth + side) * CORES + unit

    up, down = at(z + 1, y, core), at(z - 1, y, core)
    across, twin = at(z, depth - 1 - y, core), at(z, y, CORES - 1 - core)
    below, above = z > 0, z + 1 < layers

    def signal(semaphore, target):
        pl.semaphore_signal(semaphore, inc=1, device_id={"row": target}, device_id_type=MESH)

    barrier = pltpu.get_barrier_semaphore()

    @pl.loop(1, lane)
    def _(hop):
        signal(barrier, z * lane + (inner + hop) % lane)

    @pl.when(above)
    def _():
        signal(barrier, up)

    @pl.when(below)
    def _():
        signal(barrier, down)

    for load in loads:
        load.wait()
    stage[:, :SLAB] = rows[:, :SLAB]
    for obs_at in range(obs):
        value = ids[obs_at].astype(jnp.float32)
        stage[obs_at : obs_at + 1, SLAB:] = jnp.full((1, TILE), value, jnp.float32)

    def cut(ref, piece):
        return ref.at[pl.ds((piece // PARTS) * 8, 8), pl.ds((piece % PARTS) * part, part)]

    def pass_on(kind, origin, piece, target, own=False):
        return pltpu.make_async_remote_copy(
            src_ref=cut(stage if own else slab_all.at[origin], piece),
            dst_ref=cut(slab_all.at[origin], piece),
            send_sem=slab_send.at[kind, origin, piece],
            recv_sem=slab_recv.at[origin, piece],
            device_id={"row": target},
            device_id_type=MESH,
        )

    def arrived(origin, piece):
        pass_on(3, origin, piece, twin).wait_recv()

    def deal(peer):
        return pltpu.make_async_remote_copy(
            src_ref=packed.at[peer],
            dst_ref=own_all.at[me],
            send_sem=own_send.at[peer],
            recv_sem=own_recv.at[me],
            device_id={"row": peer},
            device_id_type=MESH,
        )

    def deals(layer):
        @pl.loop(0, lane)
        def _(unit):
            deal(layer * lane + unit).start()

    pl.semaphore_wait(barrier, lane - 1 + jnp.where(above, 1, 0) + jnp.where(below, 1, 0))

    @pl.when(above)
    def _():
        signal(in_below.at[z], up)

    @pl.when(below)
    def _():
        signal(in_above.at[z], down)

    for piece in range(pieces):
        @pl.when(z + 1 < layers)
        def _():
            pass_on(0, me, piece, up, True).start()

        @pl.when(z > 0)
        def _():
            pass_on(1, me, piece, down, True).start()

        if depth > 1:
            pass_on(2, me, piece, across, True).start()
        pass_on(3, me, piece, twin, True).start()
    keep = pltpu.make_async_copy(stage, slab_all.at[me], keep_sem.at[0])
    keep.start()

    @pl.loop(0, n)
    def _(peer):
        for k in range(tiles):
            column = order[peer * tiles + k] * TILE
            packed[peer, :, k * TILE : (k + 1) * TILE] = rows[:, pl.ds(column, TILE)]

    keep_own = pltpu.make_async_copy(packed.at[me], own_all.at[me], keep_sem.at[1])
    keep_own.start()

    @pl.loop(1, lane)
    def _(hop):
        deal(z * lane + (inner + hop) % lane).start()

    @pl.loop(1, layers)
    def _(s):
        @pl.when(z - s >= 0)
        def _():
            pl.semaphore_wait(in_below.at[z - s], 1)

            @pl.when(above)
            def _():
                signal(in_below.at[z - s], up)

        @pl.when(z + s < layers)
        def _():
            pl.semaphore_wait(in_above.at[z + s], 1)

            @pl.when(below)
            def _():
                signal(in_above.at[z + s], down)

        if DEALS == 1:
            @pl.when(z - s >= 0)
            def _():
                deals(z - s)

            @pl.when(z + s < layers)
            def _():
                deals(z + s)

        for piece in range(pieces):
            @pl.when(z - s >= 0)
            def _():
                origin = at(z - s, y, core)
                arrived(origin, piece)

                @pl.when(z + 1 < layers)
                def _():
                    pass_on(0, origin, piece, up).start()

                if depth > 1:
                    pass_on(2, origin, piece, across).start()
                pass_on(3, origin, piece, twin).start()

            @pl.when(z + s < layers)
            def _():
                origin = at(z + s, y, core)
                arrived(origin, piece)

                @pl.when(z > 0)
                def _():
                    pass_on(1, origin, piece, down).start()

                if depth > 1:
                    pass_on(2, origin, piece, across).start()
                pass_on(3, origin, piece, twin).start()

        if DEALS == 2:
            @pl.when(z - s >= 0)
            def _():
                deals(z - s)

            @pl.when(z + s < layers)
            def _():
                deals(z + s)

    if DEALS == 3:
        @pl.loop(1, layers)
        def _(s):
            @pl.when(z - s >= 0)
            def _():
                deals(z - s)

            @pl.when(z + s < layers)
            def _():
                deals(z + s)

    if depth > 1:
        @pl.loop(1, layers + 1)
        def _(s):
            for piece in range(pieces):
                @pl.when(z - s + 1 >= 0)
                def _():
                    origin = at(z - s + 1, depth - 1 - y, core)
                    arrived(origin, piece)
                    pass_on(3, origin, piece, twin).start()

                @pl.when(jnp.logical_and(s > 1, z + s - 1 < layers))
                def _():
                    origin = at(z + s - 1, depth - 1 - y, core)
                    arrived(origin, piece)
                    pass_on(3, origin, piece, twin).start()

    @pl.loop(0, layers)
    def _(layer):
        for side in range(depth):
            for piece in range(pieces):
                arrived(at(layer, side, CORES - 1 - core), piece)

    @pl.loop(1, n)
    def _(hop):
        peer = lax.rem(me + hop, n)
        pltpu.make_async_remote_copy(
            src_ref=packed.at[peer], dst_ref=own_all.at[peer], send_sem=own_send.at[peer],
            recv_sem=own_recv.at[peer], device_id={"row": peer}, device_id_type=MESH,
        ).wait()

    keep.wait()
    keep_own.wait()

    @pl.loop(0, layers)
    def _(layer):
        origin = at(layer, y, core)
        for piece in range(pieces):
            @pl.when(jnp.logical_and(layer <= z, z + 1 < layers))
            def _():
                pass_on(0, origin, piece, up).wait_send()

            @pl.when(jnp.logical_and(layer >= z, z > 0))
            def _():
                pass_on(1, origin, piece, down).wait_send()

            if depth > 1:
                pass_on(2, origin, piece, across).wait_send()
            for side in range(depth):
                pass_on(3, at(layer, side, core), piece, twin).wait_send()


def two(value):
    high = value.astype(jnp.bfloat16)
    return high, (value - high.astype(jnp.float32)).astype(jnp.bfloat16)


def dot(left, right, over=1):
    return lax.dot_general(
        left, right, (((over,), (0,)), ((), ())), preferred_element_type=jnp.float32
    )


def normal(id_ref, own_ref, slab_ref, out_ref, average, own_parts):
    total = own_ref.shape[0]

    @pl.when(pl.program_id(0) == 0)
    def _():
        arcs = id_ref[...]
        alike = (arcs[:, 0:1] == jnp.transpose(arcs)[0:1, :]).astype(jnp.float32)
        counts = jnp.sum(alike, axis=1, keepdims=True)
        average[...] = (alike / counts).astype(jnp.bfloat16)
        mask = alike.astype(jnp.bfloat16)
        own = own_ref[...]
        high, rest = two(own)
        middle, low = two(own - high.astype(jnp.float32))
        sums = dot(mask, low) + dot(mask, middle) + dot(mask, high)
        centered = own - sums / counts
        high, low = two(centered)
        own_parts[:total], own_parts[total : 2 * total], own_parts[2 * total :] = high, low, high

    slab = slab_ref[...]
    high, low = two(jnp.transpose(slab - dot(average[...], slab.astype(jnp.bfloat16))))
    out_ref[...] = dot(jnp.concatenate([low, high, high], axis=1), own_parts[...])


def shards(depth, design_rows, arc_ids, tile_order):
    obs, columns = design_rows.shape
    n = lax.axis_size("row")
    mine = columns // n
    total = n * obs
    pieces = obs // 8 * PARTS
    layers = n // (depth * CORES)
    slab_all, own_all = pl.pallas_call(
        functools.partial(exchange, depth),
        out_shape=(
            jax.ShapeDtypeStruct((n, obs, WIDE), jnp.float32),
            jax.ShapeDtypeStruct((n, obs, mine), jnp.float32),
        ),
        in_specs=[
            pl.BlockSpec(memory_space=pltpu.HBM),
            pl.BlockSpec(memory_space=pltpu.HBM),
            pl.BlockSpec(memory_space=pltpu.HBM),
        ],
        out_specs=(pl.BlockSpec(memory_space=pl.ANY), pl.BlockSpec(memory_space=pl.ANY)),
        scratch_shapes=[
            pltpu.SMEM(tile_order.shape, jnp.int32),
            pltpu.SMEM(arc_ids.shape, jnp.int32),
            pltpu.VMEM(design_rows.shape, jnp.float32),
            pltpu.VMEM((obs, WIDE), jnp.float32),
            pltpu.VMEM((n, obs, mine), jnp.float32),
            pltpu.SemaphoreType.DMA((n, pieces)),
            pltpu.SemaphoreType.DMA((n,)),
            pltpu.SemaphoreType.DMA((4, n, pieces)),
            pltpu.SemaphoreType.DMA((n,)),
            pltpu.SemaphoreType.DMA((3,)),
            pltpu.SemaphoreType.DMA((2,)),
            pltpu.SemaphoreType.REGULAR((layers,)),
            pltpu.SemaphoreType.REGULAR((layers,)),
        ],
        compiler_params=pltpu.CompilerParams(
            collective_id=0, has_side_effects=True, vmem_limit_bytes=60 << 20
        ),
        name="exchange",
    )(tile_order, arc_ids, design_rows)
    slab_all = slab_all.reshape(total, WIDE)
    own_all = own_all.reshape(total, mine)
    return pl.pallas_call(
        normal,
        grid=(pl.cdiv(SLAB, STEP),),
        out_shape=jax.ShapeDtypeStruct((SLAB, mine), jnp.float32),
        in_specs=[
            pl.BlockSpec((total, TILE), lambda i: (0, SLAB // TILE)),
            pl.BlockSpec((total, mine), lambda i: (0, 0)),
            pl.BlockSpec((total, STEP), lambda i: (0, i)),
        ],
        out_specs=pl.BlockSpec((STEP, mine), lambda i: (i, 0)),
        scratch_shapes=[
            pltpu.VMEM((total, total), jnp.bfloat16),
            pltpu.VMEM((3 * total, mine), jnp.bfloat16),
        ],
        compiler_params=pltpu.CompilerParams(vmem_limit_bytes=60 << 20),
        name="normal",
    )(slab_all, own_all, slab_all)


def solution(mesh):
    depth = 4 // mesh.shape["groups"]
    return jax.shard_map(
        functools.partial(shards, depth),
        mesh=mesh,
        in_specs=(P(("groups", "row"), None), P(("groups", "row")), P()),
        out_specs=P("groups", "row"),
        check_vma=False,
    )
```

time: 50.6 us -> 41.6 us (0.82)
  Pallas kernels: 47.9 us -> 41.3 us
  local copies, waits for them, and re-layouts: 2.35 us -> 0 us
    pallas_call x1, Pallas kernels: 40.1 us -> 33.6 us  [shards(): pl.pallas_call(functools.partial(exchange, depth), out_shape=(jax.ShapeDt...]
    unnamed x6 -> x0, local copies, waits for them, and re-layouts: 2.35 us -> none
where the time goes in v2:
time: 41.6 us; the launch traced here: 41.3 us
  Pallas kernels  41.3 us (99%)
    pallas_call x1, Pallas kernels, shards(): pl.pallas_call(functools.partial(exchange, depth), out_shape=(jax.ShapeDt...  33.6 us
    pallas_call x1, Pallas kernels, shards(): pl.pallas_call(normal, grid=(pl.cdiv(SLAB, STEP),), out_shape=jax.ShapeDt...  7.73 us

profile of v2, /device:TPU:0, one launch (start us, length us, event | category | flops | bytes accessed | tf_op | source)
XLA Modules:
  0.0 41.3 jit_solution(12187701459658036671)
XLA Ops:
  0.0 33.6 %exchange.1 = (f32[16,16,3072]{2,1,0:T(8,128)}, f32[16,16,512]{2,1,0:T(8,128)}) custom-call(s32[64]{0:T(128)} %order_in.1, s32[16]{0:T(128)} %ids_in.1, f32[16,8192]{1,0:T(8,128)} %rows_in.1), custom_call_target="tpu_custom_call" | custom-call | tf_op jit(solution)/shard_map/exchange/pallas_call | solution.py:310
  33.6 7.7 %normal.1 = f32[2944,512]{1,0:T(8,128)} custom-call(f32[256,3072]{1,0:T(8,128)} %bitcast.2, f32[256,512]{1,0:T(8,128)} %bitcast.4, f32[256,3072]{1,0:T(8,128)} %bitcast.3), custom_call_target="tpu_custom_call" | custom-call | tf_op jit(solution)/shard_map/normal/pallas_call | solution.py:344

commit v3 on v2

--- a/solution.py
+++ b/solution.py
@@ -10,8 +10,9 @@
 SLAB = 2944
 TILE = 128
 WIDE = SLAB + TILE
-STEP = 768
-PARTS = 2
+STEP = 1024
+PARTS = 1
+ROWS = 8
 DEALS = 2
 CORES = 2
 MESH = pl.DeviceIdType.MESH
@@ -30,7 +31,7 @@
     layers = n // lane
     z, inner = me // lane, me % lane
     y, core = inner // CORES, inner % CORES
-    halves, part = obs // 8, WIDE // PARTS
+    halves, part = obs // ROWS, WIDE // PARTS
     pieces = halves * PARTS
 
     loads = [
@@ -73,7 +74,7 @@
         stage[obs_at : obs_at + 1, SLAB:] = jnp.full((1, TILE), value, jnp.float32)
 
     def cut(ref, piece):
-        return ref.at[pl.ds((piece // PARTS) * 8, 8), pl.ds((piece % PARTS) * part, part)]
+        return ref.at[pl.ds((piece // PARTS) * ROWS, ROWS), pl.ds((piece % PARTS) * part, part)]
 
     def pass_on(kind, origin, piece, target, own=False):
         return pltpu.make_async_remote_copy(
@@ -277,27 +278,50 @@
     )
 
 
-def normal(id_ref, own_ref, slab_ref, out_ref, average, own_parts):
-    total = own_ref.shape[0]
-
-    @pl.when(pl.program_id(0) == 0)
-    def _():
-        arcs = id_ref[...]
-        alike = (arcs[:, 0:1] == jnp.transpose(arcs)[0:1, :]).astype(jnp.float32)
-        counts = jnp.sum(alike, axis=1, keepdims=True)
-        average[...] = (alike / counts).astype(jnp.bfloat16)
-        mask = alike.astype(jnp.bfloat16)
-        own = own_ref[...]
-        high, rest = two(own)
-        middle, low = two(own - high.astype(jnp.float32))
-        sums = dot(mask, low) + dot(mask, middle) + dot(mask, high)
-        centered = own - sums / counts
-        high, low = two(centered)
-        own_parts[:total], own_parts[total : 2 * total], own_parts[2 * total :] = high, low, high
-
-    slab = slab_ref[...]
-    high, low = two(jnp.transpose(slab - dot(average[...], slab.astype(jnp.bfloat16))))
-    out_ref[...] = dot(jnp.concatenate([low, high, high], axis=1), own_parts[...])
+def normal(slab_in, own_in, out_ref, arcs_buf, own_buf, slab_buf, out_buf, average, own_parts, in_sem, out_sem):
+    total = own_in.shape[0]
+    spans = [(at, min(STEP, SLAB - at)) for at in range(0, SLAB, STEP)]
+
+    def load(step):
+        at, wide = spans[step]
+        columns = pl.ds(at, wide)
+        return pltpu.make_async_copy(slab_in.at[:, columns], slab_buf.at[:, columns], in_sem.at[2 + step])
+
+    def store(step):
+        at, wide = spans[step]
+        columns = pl.ds(at, wide)
+        return pltpu.make_async_copy(out_buf.at[columns], out_ref.at[columns], out_sem.at[step])
+
+    load_arcs = pltpu.make_async_copy(slab_in.at[:, pl.ds(SLAB, TILE)], arcs_buf, in_sem.at[0])
+    load_own = pltpu.make_async_copy(own_in, own_buf, in_sem.at[1])
+    load_arcs.start()
+    load_own.start()
+    for step in range(len(spans)):
+        load(step).start()
+
+    load_arcs.wait()
+    arcs = arcs_buf[...]
+    alike = (arcs[:, 0:1] == jnp.transpose(arcs)[0:1, :]).astype(jnp.float32)
+    counts = jnp.sum(alike, axis=1, keepdims=True)
+    average[...] = (alike / counts).astype(jnp.bfloat16)
+    mask = alike.astype(jnp.bfloat16)
+    load_own.wait()
+    own = own_buf[...]
+    high = own.astype(jnp.bfloat16)
+    middle, low = two(own - high.astype(jnp.float32))
+    sums = dot(mask, low) + dot(mask, middle) + dot(mask, high)
+    high, low = two(own - sums / counts)
+    own_parts[:total], own_parts[total : 2 * total], own_parts[2 * total :] = high, low, high
+
+    for step, (at, wide) in enumerate(spans):
+        load(step).wait()
+        slab = slab_buf[:, at : at + wide]
+        high, low = two(jnp.transpose(slab - dot(average[...], slab.astype(jnp.bfloat16))))
+        out_buf[at : at + wide] = dot(jnp.concatenate([low, high, high], axis=1), own_parts[...])
+        store(step).start()
+
+    for step in range(len(spans)):
+        store(step).wait()
 
 
 def shards(depth, design_rows, arc_ids, tile_order):
@@ -305,7 +329,7 @@
     n = lax.axis_size("row")
     mine = columns // n
     total = n * obs
-    pieces = obs // 8 * PARTS
+    pieces = obs // ROWS * PARTS
     layers = n // (depth * CORES)
     slab_all, own_all = pl.pallas_call(
         functools.partial(exchange, depth),
@@ -341,23 +365,25 @@
     )(tile_order, arc_ids, design_rows)
     slab_all = slab_all.reshape(total, WIDE)
     own_all = own_all.reshape(total, mine)
+    steps = pl.cdiv(SLAB, STEP)
     return pl.pallas_call(
         normal,
-        grid=(pl.cdiv(SLAB, STEP),),
         out_shape=jax.ShapeDtypeStruct((SLAB, mine), jnp.float32),
-        in_specs=[
-            pl.BlockSpec((total, TILE), lambda i: (0, SLAB // TILE)),
-            pl.BlockSpec((total, mine), lambda i: (0, 0)),
-            pl.BlockSpec((total, STEP), lambda i: (0, i)),
-        ],
-        out_specs=pl.BlockSpec((STEP, mine), lambda i: (i, 0)),
+        in_specs=[pl.BlockSpec(memory_space=pl.ANY), pl.BlockSpec(memory_space=pl.ANY)],
+        out_specs=pl.BlockSpec(memory_space=pl.ANY),
         scratch_shapes=[
+            pltpu.VMEM((total, TILE), jnp.float32),
+            pltpu.VMEM((total, mine), jnp.float32),
+            pltpu.VMEM((total, SLAB), jnp.float32),
+            pltpu.VMEM((SLAB, mine), jnp.float32),
             pltpu.VMEM((total, total), jnp.bfloat16),
             pltpu.VMEM((3 * total, mine), jnp.bfloat16),
+            pltpu.SemaphoreType.DMA((2 + steps,)),
+            pltpu.SemaphoreType.DMA((steps,)),
         ],
         compiler_params=pltpu.CompilerParams(vmem_limit_bytes=60 << 20),
         name="normal",
-    )(slab_all, own_all, slab_all)
+    )(slab_all, own_all)
 
 
 def solution(mesh):

time: 41.6 us -> 38.8 us (0.933)
  Pallas kernels: 41.3 us -> 38.6 us
    pallas_call x1, Pallas kernels: 33.6 us -> 32.1 us  [shards(): pl.pallas_call(functools.partial(exchange, depth), out_shape=(jax.ShapeDt...]
    pallas_call x1, Pallas kernels: 7.73 us -> 6.5 us  [shards(): pl.pallas_call(normal, out_shape=jax.ShapeDtypeStruct((SLAB, mine), jnp.f...]
where the time goes in v3:
time: 38.8 us; the launch traced here: 38.6 us
  Pallas kernels  38.6 us (99%)
    pallas_call x1, Pallas kernels, shards(): pl.pallas_call(functools.partial(exchange, depth), out_shape=(jax.ShapeDt...  32.1 us
    pallas_call x1, Pallas kernels, shards(): pl.pallas_call(normal, out_shape=jax.ShapeDtypeStruct((SLAB, mine), jnp.f...  6.5 us

profile of v3, /device:TPU:0, one launch (start us, length us, event | category | flops | bytes accessed | tf_op | source)
XLA Modules:
  0.0 38.6 jit_solution(14547666674459791497)
XLA Ops:
  0.0 32.1 %exchange.1 = (f32[16,16,3072]{2,1,0:T(8,128)}, f32[16,16,512]{2,1,0:T(8,128)}) custom-call(s32[64]{0:T(128)} %order_in.1, s32[16]{0:T(128)} %ids_in.1, f32[16,8192]{1,0:T(8,128)} %rows_in.1), custom_call_target="tpu_custom_call" | custom-call | tf_op jit(solution)/shard_map/exchange/pallas_call | solution.py:334
  32.1 6.5 %normal.1 = f32[2944,512]{1,0:T(8,128)} custom-call(f32[256,3072]{1,0:T(8,128)} %bitcast.2, f32[256,512]{1,0:T(8,128)} %bitcast.3), custom_call_target="tpu_custom_call" | custom-call | tf_op jit(solution)/shard_map/normal/pallas_call | solution.py:369

commit v4 on v3

--- a/solution.py
+++ b/solution.py
@@ -13,7 +13,6 @@
 STEP = 1024
 PARTS = 1
 ROWS = 8
-DEALS = 2
 CORES = 2
 MESH = pl.DeviceIdType.MESH
 
@@ -160,15 +159,6 @@
             def _():
                 signal(in_above.at[z + s], down)
 
-        if DEALS == 1:
-            @pl.when(z - s >= 0)
-            def _():
-                deals(z - s)
-
-            @pl.when(z + s < layers)
-            def _():
-                deals(z + s)
-
         for piece in range(pieces):
             @pl.when(z - s >= 0)
             def _():
@@ -196,25 +186,15 @@
                     pass_on(2, origin, piece, across).start()
                 pass_on(3, origin, piece, twin).start()
 
-        if DEALS == 2:
-            @pl.when(z - s >= 0)
-            def _():
-                deals(z - s)
-
-            @pl.when(z + s < layers)
-            def _():
-                deals(z + s)
-
-    if DEALS == 3:
-        @pl.loop(1, layers)
-        def _(s):
-            @pl.when(z - s >= 0)
-            def _():
-                deals(z - s)
-
-            @pl.when(z + s < layers)
-            def _():
-                deals(z + s)
+        ahead, behind = layers - 1 - z, z
+
+        @pl.loop(jnp.where(s == behind, 1, s), jnp.where(s >= behind, jnp.minimum(s, ahead) + 1, 0))
+        def _(far):
+            deals(z + far)
+
+        @pl.loop(jnp.where(s == ahead, 1, s), jnp.where(s >= ahead, jnp.minimum(s, behind) + 1, 0))
+        def _(far):
+            deals(z - far)
 
     if depth > 1:
         @pl.loop(1, layers + 1)

time: 38.8 us -> 37.5 us (0.966)
  Pallas kernels: 38.6 us -> 37.2 us
    pallas_call x1, Pallas kernels: 32.1 us -> 30.7 us  [shards(): pl.pallas_call(functools.partial(exchange, depth), out_shape=(jax.ShapeDt...]
where the time goes in v4:
time: 37.5 us; the launch traced here: 37.2 us
  Pallas kernels  37.2 us (99%)
    pallas_call x1, Pallas kernels, shards(): pl.pallas_call(functools.partial(exchange, depth), out_shape=(jax.ShapeDt...  30.7 us
    pallas_call x1, Pallas kernels, shards(): pl.pallas_call(normal, out_shape=jax.ShapeDtypeStruct((SLAB, mine), jnp.f...  6.49 us

profile of v4, /device:TPU:0, one launch (start us, length us, event | category | flops | bytes accessed | tf_op | source)
XLA Modules:
  0.0 37.2 jit_solution(9401873255383410646)
XLA Ops:
  0.0 30.7 %exchange.1 = (f32[16,16,3072]{2,1,0:T(8,128)}, f32[16,16,512]{2,1,0:T(8,128)}) custom-call(s32[64]{0:T(128)} %order_in.1, s32[16]{0:T(128)} %ids_in.1, f32[16,8192]{1,0:T(8,128)} %rows_in.1), custom_call_target="tpu_custom_call" | custom-call | tf_op jit(solution)/shard_map/exchange/pallas_call | solution.py:314
  30.8 6.5 %normal.1 = f32[2944,512]{1,0:T(8,128)} custom-call(f32[256,3072]{1,0:T(8,128)} %bitcast.2, f32[256,512]{1,0:T(8,128)} %bitcast.3), custom_call_target="tpu_custom_call" | custom-call | tf_op jit(solution)/shard_map/normal/pallas_call | solution.py:349

commit v5 on v4

--- a/solution.py
+++ b/solution.py
@@ -10,7 +10,7 @@
 SLAB = 2944
 TILE = 128
 WIDE = SLAB + TILE
-STEP = 1024
+STEP = 1152
 PARTS = 1
 ROWS = 8
 CORES = 2

time: 37.5 us -> 37.4 us (level)
  no operation moved by 1% of the time
where the time goes in v5:
time: 37.4 us; the launch traced here: 37.1 us
  Pallas kernels  37.1 us (99%)
    pallas_call x1, Pallas kernels, shards(): pl.pallas_call(functools.partial(exchange, depth), out_shape=(jax.ShapeDt...  30.7 us
    pallas_call x1, Pallas kernels, shards(): pl.pallas_call(normal, out_shape=jax.ShapeDtypeStruct((SLAB, mine), jnp.f...  6.35 us

profile of v5, /device:TPU:0, one launch (start us, length us, event | category | flops | bytes accessed | tf_op | source)
XLA Modules:
  0.0 37.1 jit_solution(671217118187741886)
XLA Ops:
  0.0 30.7 %exchange.1 = (f32[16,16,3072]{2,1,0:T(8,128)}, f32[16,16,512]{2,1,0:T(8,128)}) custom-call(s32[64]{0:T(128)} %order_in.1, s32[16]{0:T(128)} %ids_in.1, f32[16,8192]{1,0:T(8,128)} %rows_in.1), custom_call_target="tpu_custom_call" | custom-call | tf_op jit(solution)/shard_map/exchange/pallas_call | solution.py:314
  30.8 6.3 %normal.1 = f32[2944,512]{1,0:T(8,128)} custom-call(f32[256,3072]{1,0:T(8,128)} %bitcast.2, f32[256,512]{1,0:T(8,128)} %bitcast.3), custom_call_target="tpu_custom_call" | custom-call | tf_op jit(solution)/shard_map/normal/pallas_call | solution.py:349
